TPU v7x, 256 devices: a whole 4x4x8 slice. The times are simulated.
256 devices in a mesh: dp: 16 (over y, z_hi), latent: 16 (over z_lo, x, core).
Axes of the slice: x: 4, y: 4, z: 8 (z_hi: 4, z_lo: 2; z = z_hi * 2 + z_lo), core: 2. Of those that a mesh axis runs over, the one named last changes fastest.
Arguments:
- activations: bfloat16 [8192, 3584], P('dp'), may hold values from -6 to 6
- w_enc: float32 [3584, 8192], P('dp', 'latent'), may hold values from -0.09375 to 0.09375
- w_dec: float32 [3584, 8192], P('dp', 'latent'), may hold values from -0.0625 to 0.0625
- b_enc: float32 [8192], P('latent'), may hold values from -3 to 3
- b_dec: float32 [3584], replicated, may hold values from -3 to 3
- m_enc: float32 [3584, 8192], P('dp', 'latent'), may hold values from -0.12 to 0.12
- v_enc: float32 [3584, 8192], P('dp', 'latent'), may hold values from 0.0001 to 0.001
- m_dec: float32 [3584, 8192], P('dp', 'latent'), may hold values from -0.12 to 0.12
- v_dec: float32 [3584, 8192], P('dp', 'latent'), may hold values from 0.0001 to 0.001
- m_b_enc: float32 [8192], P('latent'), may hold values from -0.12 to 0.12
- v_b_enc: float32 [8192], P('latent'), may hold values from 0.0001 to 0.001
- m_b_dec: float32 [3584], replicated, may hold values from -0.12 to 0.12
- v_b_dec: float32 [3584], replicated, may hold values from 0.0001 to 0.001
Outputs:
- new_w_enc: float32 [3584, 8192], P('dp', 'latent')
- new_m_enc: float32 [3584, 8192], P('dp', 'latent')
- new_v_enc: float32 [3584, 8192], P('dp', 'latent')
- new_w_dec: float32 [3584, 8192], P('dp', 'latent')
- new_m_dec: float32 [3584, 8192], P('dp', 'latent')
- new_v_dec: float32 [3584, 8192], P('dp', 'latent')
- new_b_enc: float32 [8192], P('latent')
- new_m_b_enc: float32 [8192], P('latent')
- new_v_b_enc: float32 [8192], P('latent')
- new_b_dec: float32 [3584], replicated
- new_m_b_dec: float32 [3584], replicated
- new_v_b_dec: float32 [3584], replicated
All inputs are finite; a program needn't handle non-finite values.
Results may differ from a plain program's by a relative error of at most 0.0082.
Values may be sent and summed in bfloat16 or wider, within the bound.
No kernel may reach another device: no remote copies, remote signals or barrier semaphores. Data moves between devices by JAX's collectives and lax.ppermute only.
A program may use at most 128 MiB of HBM per device.

v0:
```python
import jax
import jax.numpy as jnp
from jax import lax
from jax.sharding import PartitionSpec as P

ADAM_STEP = 100


BETA_ONE = 0.9
BETA_TWO = 0.999
LEARNING_RATE = 0.001
ADAM_EPS = 1e-08
NORM_EPS = 1e-06
SPARSITY = 5.0


def adam_step(weights, gradient, moment_one, moment_two):
    one_new = BETA_ONE * moment_one + (1.0 - BETA_ONE) * gradient
    two_new = BETA_TWO * moment_two + (1.0 - BETA_TWO) * gradient * gradient
    fix_one = 1.0 - BETA_ONE**ADAM_STEP
    fix_two = 1.0 - BETA_TWO**ADAM_STEP
    updated = weights - LEARNING_RATE * (one_new / fix_one) / (
        jnp.sqrt(two_new / fix_two) + ADAM_EPS
    )
    return (updated, one_new, two_new)


def contract_rows(left, right):
    return lax.dot_general(
        left, right, (((0,), (0,)), ((), ())), preferred_element_type=jnp.float32
    )


def latent_sum(left, right):
    return lax.dot_general(
        left, right, (((1,), (1,)), ((), ())), preferred_element_type=jnp.float32
    )


def body(
    activations,
    w_enc,
    w_dec,
    b_enc,
    b_dec,
    m_enc,
    v_enc,
    m_dec,
    v_dec,
    m_b_enc,
    v_b_enc,
    m_b_dec,
    v_b_dec,
):
    dp_count = lax.axis_size("dp")
    group_rows = activations.shape[0]
    rows_total = group_rows * dp_count
    lat_width = w_enc.shape[1]
    enc_half = w_enc.astype(jnp.bfloat16)
    dec_half = w_dec.astype(jnp.bfloat16)
    encoded = jnp.dot(
        activations,
        lax.all_gather(enc_half, "dp", axis=0, tiled=True),
        preferred_element_type=jnp.float32,
    )
    preacts = encoded + b_enc
    dec_full = lax.all_gather(dec_half, "dp", axis=0, tiled=True)
    features = jnp.maximum(preacts, 0.0).astype(jnp.bfloat16)
    dec_wide = dec_full.astype(jnp.float32)
    col_norms = jnp.sqrt(jnp.sum(dec_wide * dec_wide, axis=0) + NORM_EPS)
    scaling = 2.0 / rows_total
    penalty = SPARSITY / rows_total
    rebuilt = lax.psum(latent_sum(features, dec_full), "latent")
    grad_out = ((rebuilt + b_dec - activations.astype(jnp.float32)) * scaling).astype(jnp.bfloat16)
    grad_feat = (
        jnp.dot(grad_out, dec_full, preferred_element_type=jnp.float32) + penalty * col_norms
    )
    grad_pre = jnp.where(preacts > 0.0, grad_feat, 0.0).astype(jnp.bfloat16)
    bias_out_part = jnp.sum(grad_out.astype(jnp.float32), axis=0)
    own_totals = jnp.sum(features.astype(jnp.float32), axis=0)
    weighted = penalty * own_totals / col_norms
    enc_term = contract_rows(activations, grad_pre)
    dec_term = contract_rows(grad_out, features) + weighted * dec_wide
    both_grads = lax.psum_scatter(
        jnp.concatenate([enc_term, dec_term], axis=1), "dp", scatter_dimension=0, tiled=True
    )
    grad_w_enc = both_grads[:, :lat_width]
    grad_w_dec = both_grads[:, lat_width:]
    grad_b_enc_part = jnp.sum(grad_pre.astype(jnp.float32), axis=0)
    grad_b_dec, grad_b_enc = lax.psum((bias_out_part, grad_b_enc_part), "dp")
    new_w_enc, new_m_enc, new_v_enc = adam_step(w_enc, grad_w_enc, m_enc, v_enc)
    new_w_dec, new_m_dec, new_v_dec = adam_step(w_dec, grad_w_dec, m_dec, v_dec)
    new_b_enc, new_m_b_enc, new_v_b_enc = adam_step(b_enc, grad_b_enc, m_b_enc, v_b_enc)
    new_b_dec, new_m_b_dec, new_v_b_dec = adam_step(b_dec, grad_b_dec, m_b_dec, v_b_dec)
    return (
        new_w_enc,
        new_m_enc,
        new_v_enc,
        new_w_dec,
        new_m_dec,
        new_v_dec,
        new_b_enc,
        new_m_b_enc,
        new_v_b_enc,
        new_b_dec,
        new_m_b_dec,
        new_v_b_dec,
    )


def solution(mesh):
    in_specs = (
        P("dp", None),
        P("dp", "latent"),
        P("dp", "latent"),
        P("latent"),
        P(),
        P("dp", "latent"),
        P("dp", "latent"),
        P("dp", "latent"),
        P("dp", "latent"),
        P("latent"),
        P("latent"),
        P(),
        P(),
    )
    out_specs = (
        P("dp", "latent"),
        P("dp", "latent"),
        P("dp", "latent"),
        P("dp", "latent"),
        P("dp", "latent"),
        P("dp", "latent"),
        P("latent"),
        P("latent"),
        P("latent"),
        P(),
        P(),
        P(),
    )
    return jax.shard_map(body, mesh=mesh, in_specs=in_specs, out_specs=out_specs, check_vma=False)
```

profile of v0, /device:TPU:121, one launch (start us, length us, event | category | flops | bytes accessed | tf_op | source)
XLA Modules:
  0.0 537.3 jit_solution(12880455971813270375)
XLA Ops:
  7.2 0.0 all-gather.3.cloned.1.call-start
  7.2 1.7 convert_element_type.30
  9.0 0.0 all-gather.3.cloned.1.call-update
  9.0 0.0 all-gather.5.cloned.1.call-start
  9.0 1.7 convert_element_type.32
  10.8 0.0 all-gather.5.cloned.1.call-update
  10.8 0.0 all-reduce.3.cloned.1.call-start
  10.8 72.9 %all-gather.3.cloned.1.call-done = bf16[3584,512]{1,0:T(8,128)(2,1)} async-done(((bf16[224,512]{1,0:T(8,128)(2,1)}), bf16[3584,512]{1,0:T(8,128)(2,1)}) %all-gather.3.cloned.1.call-update) | async-done | bytes 3670032 | tf_op jit(solution)/shard_map/all_gather | solution.py:63
  83.8 5.2 convert_reduce_fusion.2
  89.0 68.3 %all-gather.5.cloned.1.call-done = bf16[3584,512]{1,0:T(8,128)(2,1)} async-done(((bf16[224,512]{1,0:T(8,128)(2,1)}), bf16[3584,512]{1,0:T(8,128)(2,1)}) %all-gather.5.cloned.1.call-update) | async-done | bytes 3670032 | tf_op jit(solution)/shard_map/all_gather | solution.py:67
  157.3 7.2 %fusion.8 = f32[512,3584]{1,0:T(8,128)} fusion(bf16[3584,512]{1,0:T(8,128)(2,1)} %all-gather.5.cloned.1.call-done, f32[512,512]{1,0:T(8,128)S(1)} %get-tuple-element.58), kind=kOutput, calls=%fused_computation.33 | convolution fusion | flops 1879572480 | bytes 12058624 | tf_op jit(solution)/shard_map/dot_general | solution.py:35
  164.4 0.0 all-reduce.3.cloned.1.call-update
  164.5 0.0 reduce-scatter.4.cloned.1.call-start
  164.5 6.0 %copy.51 = bf16[3584,512]{0,1:T(8,128)(2,1)} copy(bf16[3584,512]{1,0:T(8,128)(2,1)} %all-gather.5.cloned.1.call-done) | data formatting | bytes 7340032 | tf_op jit(solution)/shard_map/all_gather | solution.py:67
  170.5 2.8 fusion
  173.4 132.4 %all-reduce.3.cloned.1.call-done = f32[512,3584]{1,0:T(8,128)} async-done(((f32[512,3584]{1,0:T(8,128)}), f32[512,3584]{1,0:T(8,128)}) %all-reduce.3.cloned.1.call-update) | async-done | bytes 7340048 | tf_op jit(solution)/shard_map/psum | solution.py:73
  305.8 5.8 %convert_reduce_fusion = (f32[3584]{0:T(1024)S(1)}, bf16[512,3584]{1,0:T(8,128)(2,1)S(1)}) fusion(bf16[512,3584]{1,0:T(8,128)(2,1)} %param.13, f32[512,3584]{1,0:T(8,128)} %all-reduce.3.cloned.1.call-done, f32[3584]{0:T(1024)S(1)} %copy-done.9), kind=kLoop, calls=%fused_computation.5 | loop fusion | flops 12841472 | bytes 14708736 | tf_op jit(solution)/shard_map/reduce_sum | solution.py:79
  311.7 2.1 convert_reduce_fusion.1
  313.8 2.1 convolution_bitcast_fusion
  315.9 2.2 fusion.1
  318.0 5.5 %pad_maximum_fusion = f32[3584,1024]{0,1:T(8,128)} fusion(f32[3584,512]{0,1:T(8,128)S(1)} %fusion.1, f32[3584,512]{0,1:T(8,128)S(1)} %convolution_bitcast_fusion), kind=kLoop, calls=%fused_computation | loop fusion | flops 3670016 | bytes 29360128 | tf_op jit(solution)/shard_map/concatenate | solution.py:85
  323.6 15.3 %copy.54 = f32[3584,1024]{1,0:T(8,128)} copy(f32[3584,1024]{0,1:T(8,128)} %pad_maximum_fusion) | data formatting | bytes 29360128
  338.9 0.0 copy-start.11
  338.9 0.0 copy-start.4
  338.9 0.0 copy-start.5
  339.0 0.0 copy-start.8
  339.0 0.0 reduce-scatter.4.cloned.1.call-update
  339.0 76.4 %all-reduce = (f32[512]{0:T(512)S(1)}, f32[3584]{0:T(1024)S(1)}) all-reduce(f32[512]{0:T(512)S(1)} %get-tuple-element.59, f32[3584]{0:T(1024)S(1)} %get-tuple-element.44), channel_id=1, replica_groups=mesh['dp'=16,'latent'=16] {'dp'}, use_global_device_ids=true, to_apply=%region_5.6 | all-reduce | flops 4096 | bytes 32768 | tf_op jit(solution)/shard_map/psum | solution.py:90
  415.5 0.6 divide_subtract_fusion.3
  416.1 0.6 divide_subtract_fusion.2
  416.7 110.9 %reduce-scatter.4.cloned.1.call-done = f32[224,1024]{1,0:T(8,128)} async-done(((f32[3584,1024]{1,0:T(8,128)}), f32[224,1024]{1,0:T(8,128)}) %reduce-scatter.4.cloned.1.call-update) | async-done | bytes 917520 | tf_op jit(solution)/shard_map/reduce_scatter | solution.py:84
  527.6 3.1 divide_subtract_fusion
  (27 shorter events, 0.1 us)
Async XLA Ops:
  7.2 76.6 %all-gather.3.cloned.1.call-start = ((), (), s32[]{:S(2)}) async-start(), calls=%async_computation.1 | async-start | bytes 3899392 | tf_op jit(solution)/shard_map/all_gather | solution.py:63
  9.0 148.3 %all-gather.5.cloned.1.call-start = ((), (), s32[]{:S(2)}) async-start(), calls=%async_computation.2 | async-start | bytes 3899392 | tf_op jit(solution)/shard_map/all_gather | solution.py:67
  10.8 295.0 %all-reduce.3.cloned.1.call-start = ((), (), s32[]{:S(2)}) async-start(), calls=%async_computation.3 | async-start | bytes 14680064 | tf_op jit(solution)/shard_map/psum | solution.py:73
  164.5 363.1 %reduce-scatter.4.cloned.1.call-start = ((), (), s32[]{:S(2)}) async-start(), calls=%async_computation.4 | async-start | bytes 15597568 | tf_op jit(solution)/shard_map/reduce_scatter | solution.py:84
  170.5 135.3 %copy-start.9 = (f32[3584]{0:T(1024)S(1)}, f32[3584]{0:T(1024)}, u32[]{:S(2)}) copy-start(f32[3584]{0:T(1024)} %param.17) | copy-start | bytes 43012
  305.8 5.8 %copy-start.2 = (bf16[3584,512]{1,0:T(8,128)(2,1)S(1)}, bf16[3584,512]{1,0:T(8,128)(2,1)}, u32[]{:S(2)}) copy-start(bf16[3584,512]{1,0:T(8,128)(2,1)} %all-gather.5.cloned.1.call-done) | copy-start | bytes 11010052
  311.6 2.1 copy-start.1
  313.8 2.1 copy-start
  338.9 76.6 %copy-start.12 = (f32[512]{0:T(512)S(1)}, f32[512]{0:T(512)}, u32[]{:S(2)}) copy-start(f32[512]{0:T(512)} %param.16) | copy-start | bytes 6148
  338.9 76.6 %copy-start.13 = (f32[512]{0:T(512)S(1)}, f32[512]{0:T(512)}, u32[]{:S(2)}) copy-start(f32[512]{0:T(512)} %param.22) | copy-start | bytes 6148
  338.9 76.6 %copy-start.14 = (f32[512]{0:T(512)S(1)}, f32[512]{0:T(512)}, u32[]{:S(2)}) copy-start(f32[512]{0:T(512)} %param.23) | copy-start | bytes 6148
  338.9 77.2 %copy-start.10 = (f32[3584]{0:T(1024)S(1)}, f32[3584]{0:T(1024)}, u32[]{:S(2)}) copy-start(f32[3584]{0:T(1024)} %param.24) | copy-start | bytes 43012
  338.9 77.2 %copy-start.11 = (f32[3584]{0:T(1024)S(1)}, f32[3584]{0:T(1024)}, u32[]{:S(2)}) copy-start(f32[3584]{0:T(1024)} %param.25) | copy-start | bytes 43012
  338.9 188.7 %copy-start.3 = (f32[224,512]{1,0:T(8,128)S(1)}, f32[224,512]{1,0:T(8,128)}, u32[]{:S(2)}) copy-start(f32[224,512]{1,0:T(8,128)} %param.15) | copy-start | bytes 1376260
  338.9 188.7 %copy-start.4 = (f32[224,512]{1,0:T(8,128)S(1)}, f32[224,512]{1,0:T(8,128)}, u32[]{:S(2)}) copy-start(f32[224,512]{1,0:T(8,128)} %param.14) | copy-start | bytes 1376260
  338.9 188.7 %copy-start.5 = (f32[224,512]{1,0:T(8,128)S(1)}, f32[224,512]{1,0:T(8,128)}, u32[]{:S(2)}) copy-start(f32[224,512]{1,0:T(8,128)} %param.20) | copy-start | bytes 1376260
  338.9 188.7 %copy-start.6 = (f32[224,512]{1,0:T(8,128)S(1)}, f32[224,512]{1,0:T(8,128)}, u32[]{:S(2)}) copy-start(f32[224,512]{1,0:T(8,128)} %param.21) | copy-start | bytes 1376260
  339.0 188.7 %copy-start.7 = (f32[224,512]{1,0:T(8,128)S(1)}, f32[224,512]{1,0:T(8,128)}, u32[]{:S(2)}) copy-start(f32[224,512]{1,0:T(8,128)} %param.19) | copy-start | bytes 1376260
  339.0 188.7 %copy-start.8 = (f32[224,512]{1,0:T(8,128)S(1)}, f32[224,512]{1,0:T(8,128)}, u32[]{:S(2)}) copy-start(f32[224,512]{1,0:T(8,128)} %param.18) | copy-start | bytes 1376260
Sparse Core Ops, SparseCore 0:
  11.1 72.6 all-gather.2
  86.8 70.4 all-gather.4
  164.6 141.1 all-reduce.2
  339.1 188.4 reduce-scatter.3
where the time goes:
time: 541 us; the launch traced here: 537 us
  waiting for transfers between devices  385 us (71%)
  blocking collectives  76.4 us (14%)
  other arithmetic  22 us (4%)
  local copies, waits for them, and re-layouts  21.4 us (4%)
  matrix products  18.7 us (3%)
  between operations  13.9 us (3%)
    psum x1, waiting for transfers between devices, body(): rebuilt = lax.psum(latent_sum(features, dec_full), 'latent')  132 us
    reduce_scatter x1, waiting for transfers between devices, body(): lax.psum_scatter(jnp.concatenate([enc_term, dec_term], axis=1), 'dp', sca...  111 us
    psum x1, blocking collectives, body(): grad_b_dec, grad_b_enc = lax.psum((bias_out_part, grad_b_enc_part), 'dp')  76.4 us
    all_gather x1, waiting for transfers between devices, body(): lax.all_gather(enc_half, 'dp', axis=0, tiled=True)  72.9 us
    all_gather x1, waiting for transfers between devices, body(): dec_full = lax.all_gather(dec_half, 'dp', axis=0, tiled=True)  68.3 us
    unnamed x31, local copies, waits for them, and re-layouts  15.4 us
  transfers between devices with their start and end apart: 4, of which 4 were waited for; matrix products, arithmetic and copies ran while one was open for 3% of the time, Pallas kernels for 0%

commit v1 on v0

v1 whole, which is shorter than its diff:
```python
import jax
import jax.numpy as jnp
from jax import lax
from jax.sharding import PartitionSpec as P

ADAM_STEP = 100


BETA_ONE = 0.9
BETA_TWO = 0.999
LEARNING_RATE = 0.001
ADAM_EPS = 1e-08
NORM_EPS = 1e-06
SPARSITY = 5.0

HALF = jnp.bfloat16
WIDE = jnp.float32

Y, Z = 4, 4
GROUPS = 8


def adam_step(weights, gradient, moment_one, moment_two):
    one_new = BETA_ONE * moment_one + (1.0 - BETA_ONE) * gradient
    two_new = BETA_TWO * moment_two + (1.0 - BETA_TWO) * gradient * gradient
    fix_one = 1.0 - BETA_ONE**ADAM_STEP
    fix_two = 1.0 - BETA_TWO**ADAM_STEP
    updated = weights - LEARNING_RATE * (one_new / fix_one) / (
        jnp.sqrt(two_new / fix_two) + ADAM_EPS
    )
    return (updated, one_new, two_new)


def dot(left, right, left_dim, right_dim):
    return lax.dot_general(
        left, right, (((left_dim,), (right_dim,)), ((), ())), preferred_element_type=WIDE
    )


def send_y(x, step):
    return lax.ppermute(x, "dp", [(s, (s // Z + step) % Y * Z + s % Z) for s in range(Y * Z)])


def send_z(x, step):
    return lax.ppermute(x, "dp", [(s, s // Z * Z + (s % Z + step) % Z) for s in range(Y * Z)])


def swap_core(x):
    return lax.ppermute(x, "latent", [(s, s ^ 1) for s in range(2 * GROUPS)])


def to_groups(x):
    return lax.all_to_all(
        x,
        "latent",
        split_axis=0,
        concat_axis=0,
        tiled=True,
        axis_index_groups=[[c + 2 * g for g in range(GROUPS)] for c in range(2)],
    )


def rows_at(x, start, count):
    return lax.dynamic_slice_in_dim(x, start, count, axis=0)


def put_rows(x, part, start):
    return lax.dynamic_update_slice_in_dim(x, part, start, axis=0)


def split_wide(x):
    high = lax.reduce_precision(x, 8, 7)
    return high.astype(HALF), (x - high).astype(HALF)


def body(
    activations,
    w_enc,
    w_dec,
    b_enc,
    b_dec,
    m_enc,
    v_enc,
    m_dec,
    v_dec,
    m_b_enc,
    v_b_enc,
    m_b_dec,
    v_b_dec,
):
    group_rows, width = activations.shape
    rows_total = group_rows * Y * Z
    own_rows, lat_width = w_enc.shape
    y_rows = own_rows * Z
    core_rows = width // 2
    slice_rows = core_rows // GROUPS
    dp_at, lat_at = lax.axis_index("dp"), lax.axis_index("latent")
    y_at, z_at = dp_at // Z, dp_at % Z
    group_at, core_at = lat_at // 2, lat_at % 2
    scaling = 2.0 / rows_total
    penalty = SPARSITY / rows_total

    def y_off(step):
        return (y_at + step) % Y * y_rows

    def z_off(step):
        return (z_at + step) % Z * own_rows

    enc_half = w_enc.astype(HALF)
    dec_half = w_dec.astype(HALF)
    dec_full = lax.all_gather(dec_half, "dp", axis=0, tiled=True)

    block = jnp.zeros((y_rows, lat_width), HALF)
    block = put_rows(block, enc_half, z_off(0))
    for step in (1, -1, 2):
        block = put_rows(block, send_z(enc_half, -step), z_off(step))
    blocks = {0: block}
    for step in (1, -1, 2):
        blocks[step] = send_y(block, -step)
    preacts = b_enc[None, :]
    for step in (0, 1, -1, 2):
        part = lax.dynamic_slice_in_dim(activations, y_off(step), y_rows, axis=1)
        preacts = preacts + dot(part, blocks[step], 1, 0)
    features = jnp.maximum(preacts, 0.0).astype(HALF)
    act_t = activations.T

    mine, other = core_at * core_rows, (1 - core_at) * core_rows
    dec_mine, dec_other = rows_at(dec_full, mine, core_rows), rows_at(dec_full, other, core_rows)
    away = swap_core(dot(dec_other, features, 1, 1).astype(HALF))
    pair = (dot(dec_mine, features, 1, 1) + away.astype(WIDE)).astype(HALF)
    parts = to_groups(pair).reshape(GROUPS, slice_rows, group_rows)
    rebuilt = jnp.sum(parts.astype(WIDE), axis=0)
    at = mine + group_at * slice_rows
    bias = lax.dynamic_slice_in_dim(b_dec, at, slice_rows)[:, None]
    out_slice = (
        (rebuilt + bias - rows_at(act_t, at, slice_rows).astype(WIDE)) * scaling
    ).astype(HALF)
    out_mine = to_groups(
        jnp.broadcast_to(out_slice[None], (GROUPS, slice_rows, group_rows)).reshape(
            core_rows, group_rows
        )
    )
    out_other = swap_core(out_mine)

    dec_wide = dec_full.astype(WIDE)
    col_norms = jnp.sqrt(jnp.sum(dec_wide * dec_wide, axis=0) + NORM_EPS)
    totals = jnp.sum(features.astype(WIDE), axis=0)
    weighted = penalty * totals / col_norms

    grad_feat = dot(out_mine, dec_mine, 0, 0) + penalty * col_norms
    grad_feat = grad_feat + dot(out_other, dec_other, 0, 0)
    grad_pre = jnp.where(preacts > 0.0, grad_feat, 0.0).astype(HALF)
    out_t = put_rows(jnp.zeros((width, group_rows), HALF), out_mine, mine)
    out_t = put_rows(out_t, out_other, other)

    bias_parts = jnp.concatenate(
        [
            jnp.sum(grad_pre.astype(WIDE), axis=0),
            jnp.sum(out_t.astype(WIDE), axis=1),
        ]
    ).reshape(-1, lat_width)
    bias_rows = bias_parts.shape[0]

    def dec_block(step):
        at = y_off(step)
        return dot(rows_at(out_t, at, y_rows), features, 1, 0) + weighted * rows_at(
            dec_full, at, y_rows
        ).astype(WIDE)

    def enc_block(step):
        return dot(rows_at(act_t, y_off(step), y_rows), grad_pre, 1, 0)

    def with_bias(x, sums):
        return jnp.concatenate([x.astype(HALF), *split_wide(sums)], axis=0)

    def unpack(x):
        x = x.astype(WIDE)
        n = x.shape[0] - 2 * bias_rows
        return x[:n], x[n : n + bias_rows] + x[n + bias_rows :]

    dec_sum = dec_block(0)
    for step in (1, -1, 2):
        dec_sum = dec_sum + send_y(dec_block(step).astype(HALF), step).astype(WIDE)
    grad_w_dec = rows_at(dec_sum, z_off(0), own_rows)
    for step in (1, -1, 2):
        piece = rows_at(dec_sum, z_off(step), own_rows).astype(HALF)
        grad_w_dec = grad_w_dec + send_z(piece, step).astype(WIDE)

    enc_sum, bias_sum = enc_block(0), bias_parts
    for step in (1, -1, 2):
        got, sums = unpack(send_y(with_bias(enc_block(step), bias_parts), step))
        enc_sum, bias_sum = enc_sum + got, bias_sum + sums
    grad_w_enc, bias_all = rows_at(enc_sum, z_off(0), own_rows), bias_sum
    for step in (1, -1, 2):
        piece = rows_at(enc_sum, z_off(step), own_rows)
        got, sums = unpack(send_z(with_bias(piece, bias_sum), step))
        grad_w_enc, bias_all = grad_w_enc + got, bias_all + sums
    bias_all = bias_all.reshape(-1)
    grad_b_enc, grad_b_dec = bias_all[:lat_width], bias_all[lat_width:]

    new_w_enc, new_m_enc, new_v_enc = adam_step(w_enc, grad_w_enc, m_enc, v_enc)
    new_w_dec, new_m_dec, new_v_dec = adam_step(w_dec, grad_w_dec, m_dec, v_dec)
    new_b_enc, new_m_b_enc, new_v_b_enc = adam_step(b_enc, grad_b_enc, m_b_enc, v_b_enc)
    new_b_dec, new_m_b_dec, new_v_b_dec = adam_step(b_dec, grad_b_dec, m_b_dec, v_b_dec)
    return (
        new_w_enc,
        new_m_enc,
        new_v_enc,
        new_w_dec,
        new_m_dec,
        new_v_dec,
        new_b_enc,
        new_m_b_enc,
        new_v_b_enc,
        new_b_dec,
        new_m_b_dec,
        new_v_b_dec,
    )


def solution(mesh):
    full, lat, rep = P("dp", "latent"), P("latent"), P()
    in_specs = (P("dp", None), full, full, lat, rep, full, full, full, full, lat, lat, rep, rep)
    out_specs = (full, full, full, full, full, full, lat, lat, lat, rep, rep, rep)
    return jax.shard_map(body, mesh=mesh, in_specs=in_specs, out_specs=out_specs, check_vma=False)
```

time: 541 us -> 311 us (0.57)
  waiting for transfers between devices: 385 us -> 193 us
  blocking collectives: 76.4 us -> 25.7 us
  starting transfers between devices: 0.16 us -> 34.9 us
  local copies, waits for them, and re-layouts: 21.4 us -> 2.58 us
  other arithmetic: 22 us -> 10.7 us
  matrix products: 18.7 us -> 25.7 us
    ppermute x0 -> x20, waiting for transfers between devices: none -> 149 us  [the longest x9 109 us: send_y(): lax.ppermute(x, 'dp', [(s, (s // Z + step) % Y * Z + s % Z) for s in rang...]
    psum x1 -> x0, waiting for transfers between devices: 132 us -> none  [body(): rebuilt = lax.psum(latent_sum(features, dec_full), 'latent')]
    reduce_scatter x1 -> x0, waiting for transfers between devices: 111 us -> none  [body(): lax.psum_scatter(jnp.concatenate([enc_term, dec_term], axis=1), 'dp', sca...]
    psum x1 -> x0, blocking collectives: 76.4 us -> none  [body(): grad_b_dec, grad_b_enc = lax.psum((bias_out_part, grad_b_enc_part), 'dp')]
    all_gather x1 -> x0, waiting for transfers between devices: 72.9 us -> none  [body(): lax.all_gather(enc_half, 'dp', axis=0, tiled=True)]
    all_gather x1, waiting for transfers between devices: 68.3 us -> 22.7 us  [body(): dec_full = lax.all_gather(dec_half, 'dp', axis=0, tiled=True)]
    ppermute x0 -> x20, starting transfers between devices: none -> 29.5 us  [the longest x9 18.1 us: send_z(): lax.ppermute(x, 'dp', [(s, s // Z * Z + (s % Z + step) % Z) for s in rang...]
    all_to_all x0 -> x1, blocking collectives: none -> 25.7 us  [to_groups(): lax.all_to_all(x, 'latent', split_axis=0, concat_axis=0, tiled=True, axis...]
  transfers between devices with their start and end apart: 4 -> 22, of which waited for: 4 -> 16; matrix products, arithmetic and copies ran while one was open for 3% -> 6% of each run, Pallas kernels for 0% -> 0%
where the time goes in v1:
time: 311 us; the launch traced here: 307 us
  waiting for transfers between devices  193 us (62%)
  starting transfers between devices  34.9 us (11%)
  matrix products  25.7 us (8%)
  blocking collectives  25.7 us (8%)
  between operations  14.6 us (5%)
  other arithmetic  10.7 us (3%)
    ppermute x9, waiting for transfers between devices, send_y(): lax.ppermute(x, 'dp', [(s, (s // Z + step) % Y * Z + s % Z) for s in rang...  109 us
    ppermute x9, waiting for transfers between devices, send_z(): lax.ppermute(x, 'dp', [(s, s // Z * Z + (s % Z + step) % Z) for s in rang...  34.5 us
    all_to_all x1, blocking collectives, to_groups(): lax.all_to_all(x, 'latent', split_axis=0, concat_axis=0, tiled=True, axis...  25.7 us
    dot_general x16, matrix products, dot(): lax.dot_general(left, right, (((left_dim,), (right_dim,)), ((), ())), pre...  25.7 us
    all_gather x1, waiting for transfers between devices, body(): dec_full = lax.all_gather(dec_half, 'dp', axis=0, tiled=True)  22.7 us
    all_to_all x1, waiting for transfers between devices, to_groups(): lax.all_to_all(x, 'latent', split_axis=0, concat_axis=0, tiled=True, axis...  21.7 us
    ppermute x9, starting transfers between devices, send_z(): lax.ppermute(x, 'dp', [(s, s // Z * Z + (s % Z + step) % Z) for s in rang...  18.1 us
    ppermute x9, starting transfers between devices, send_y(): lax.ppermute(x, 'dp', [(s, (s // Z + step) % Y * Z + s % Z) for s in rang...  8.45 us
  transfers between devices with their start and end apart: 22, of which 16 were waited for; matrix products, arithmetic and copies ran while one was open for 6% of the time, Pallas kernels for 0%

profile of v1, /device:TPU:121, one launch (start us, length us, event | category | flops | bytes accessed | tf_op | source)
XLA Modules:
  0.0 307.3 jit_solution(10314288475795425827)
XLA Ops:
  9.3 3.6 %collective-permute-start.1 = (bf16[224,512]{1,0:T(8,128)(2,1)S(1)}, bf16[224,512]{1,0:T(8,128)(2,1)S(1)}, u32[]{:S(2)}, u32[]{:S(2)}) collective-permute-start(bf16[224,512]{1,0:T(8,128)(2,1)S(1)} %get-tuple-element.29), channel_id=1, source_target_pairs={{0,16},{16,32},{32,48},{48,0},{64,80},{80,96},{96,112},{112,64},{1... | collective-permute-start | bytes 688136 | tf_op jit(solution)/shard_map/ppermute | solution.py:45
  12.9 4.2 %collective-permute-start.2 = (bf16[224,512]{1,0:T(8,128)(2,1)S(1)}, bf16[224,512]{1,0:T(8,128)(2,1)S(1)}, u32[]{:S(2)}, u32[]{:S(2)}) collective-permute-start(bf16[224,512]{1,0:T(8,128)(2,1)S(1)} %get-tuple-element.29), channel_id=1, source_target_pairs={{0,32},{16,48},{32,0},{48,16},{64,96},{80,112},{96,64},{112,80},{1... | collective-permute-start | bytes 688136 | tf_op jit(solution)/shard_map/ppermute | solution.py:45
  17.1 2.8 collective-permute-done
  19.9 12.8 %collective-permute-done.1 = bf16[224,512]{1,0:T(8,128)(2,1)S(1)} collective-permute-done((bf16[224,512]{1,0:T(8,128)(2,1)S(1)}, bf16[224,512]{1,0:T(8,128)(2,1)S(1)}, u32[]{:S(2)}, u32[]{:S(2)}) %collective-permute-start.1) | collective-permute-done | bytes 229408 | tf_op jit(solution)/shard_map/ppermute | solution.py:45
  33.9 1.9 collective-permute-start.4
  35.7 21.3 %collective-permute-done.5 = bf16[896,512]{1,0:T(8,128)(2,1)} collective-permute-done((bf16[896,512]{1,0:T(8,128)(2,1)S(1)}, bf16[896,512]{1,0:T(8,128)(2,1)}, u32[]{:S(2)}, u32[]{:S(2)}) %collective-permute-start.5) | collective-permute-done | bytes 917536 | tf_op jit(solution)/shard_map/ppermute | solution.py:41
  57.0 2.3 fusion.24
  59.3 16.6 %collective-permute-done.4 = bf16[896,512]{1,0:T(8,128)(2,1)S(1)} collective-permute-done((bf16[896,512]{1,0:T(8,128)(2,1)S(1)}, bf16[896,512]{1,0:T(8,128)(2,1)S(1)}, u32[]{:S(2)}, u32[]{:S(2)}) %collective-permute-start.4) | collective-permute-done | bytes 917536 | tf_op jit(solution)/shard_map/ppermute | solution.py:41
  75.9 1.9 fusion.27
  77.8 3.5 %collective-permute-done.3 = bf16[896,512]{1,0:T(8,128)(2,1)S(1)} collective-permute-done((bf16[896,512]{1,0:T(8,128)(2,1)S(1)}, bf16[896,512]{1,0:T(8,128)(2,1)S(1)}, u32[]{:S(2)}, u32[]{:S(2)}) %collective-permute-start.3) | collective-permute-done | bytes 917536 | tf_op jit(solution)/shard_map/ppermute | solution.py:41
  82.9 22.7 %all-gather.2.cloned.1.call-done = bf16[3584,512]{1,0:T(8,128)(2,1)} async-done(((bf16[224,512]{1,0:T(8,128)(2,1)}), bf16[3584,512]{1,0:T(8,128)(2,1)}) %all-gather.2.cloned.1.call-update) | async-done | bytes 3670032 | tf_op jit(solution)/shard_map/all_gather | solution.py:111
  105.6 3.9 %convolution_convert_fusion = bf16[1792,512]{1,0:T(8,128)(2,1)} fusion(bf16[512,512]{1,0:T(8,128)(2,1)S(1)} %get-tuple-element.22, bf16[3584,512]{1,0:T(8,128)(2,1)} %all-gather.2.cloned.1.call-done, s32[]{:T(128)S(6)} %select_n.162), kind=kOutput, calls=%fused_computation.4 | convolution fusion | flops 940441600 | bytes 4194308 | tf_op jit(solution)/shard_map/dot_general | solution.py:35
  110.0 3.8 %collective-permute-done.6 = bf16[1792,512]{1,0:T(8,128)(2,1)} collective-permute-done((bf16[1792,512]{1,0:T(8,128)(2,1)}, bf16[1792,512]{1,0:T(8,128)(2,1)}, u32[]{:S(2)}, u32[]{:S(2)}) %collective-permute-start.6) | collective-permute-done | bytes 1835040 | tf_op jit(solution)/shard_map/ppermute | solution.py:49
  113.8 4.4 %add_convert_fusion = bf16[1792,512]{1,0:T(8,128)(2,1)} fusion(bf16[1792,512]{1,0:T(8,128)(2,1)} %collective-permute-done.6, bf16[512,512]{1,0:T(8,128)(2,1)S(1)} %get-tuple-element.22, bf16[3584,512]{1,0:T(8,128)(2,1)} %all-gather.2.cloned.1.call-done, s32[]{:T(128)S(6)} %select_n.161), kind=kOutput, calls=%fused_computation.3 | convolution fusion | flops 942276608 | bytes 6029316 | tf_op jit(solution)/shard_map/dot_general | solution.py:35
  118.2 5.4 %all-to-all-start = ((bf16[8,224,512]{2,1,0:T(8,128)(2,1)}), bf16[8,224,512]{2,1,0:T(8,128)(2,1)S(1)}, u32[]{:S(2)}, u32[]{:S(2)}) async-start(bf16[8,224,512]{2,1,0:T(8,128)(2,1)} %bitcast.28), calls=%async_computation | async-start | bytes 3670016 | tf_op jit(solution)/shard_map/all_to_all | solution.py:53
  125.0 21.7 %all-to-all-done = bf16[8,224,512]{2,1,0:T(8,128)(2,1)S(1)} async-done(((bf16[8,224,512]{2,1,0:T(8,128)(2,1)}), bf16[8,224,512]{2,1,0:T(8,128)(2,1)S(1)}, u32[]{:S(2)}, u32[]{:S(2)}) %all-to-all-start) | async-done | bytes 1835040 | tf_op jit(solution)/shard_map/all_to_all | solution.py:53
  147.3 25.7 %all_to_all.18 = bf16[8,224,512]{2,1,0:T(8,128)(2,1)S(1)} all-to-all(bf16[8,224,512]{2,1,0:T(8,128)(2,1)S(1)} %broadcast_in_dim.8), channel_id=1, replica_groups={{0,2,4,6,8,10,12,14},{1,3,5,7,9,11,13,15},{16,18,20,22,24,26,28,30},{17..., dimensions={0} | all-to-all | bytes 3670016 | tf_op jit(solution)/shard_map/all_to_all | solution.py:53
  173.1 2.4 collective-permute-start.7
  180.9 1.9 convolution_convert_fusion.3
  182.9 2.2 add_convert_fusion.1
  188.9 2.7 collective-permute-start.14
  194.5 13.8 %collective-permute-done.16 = bf16[896,512]{1,0:T(8,128)(2,1)S(1)} collective-permute-done((bf16[896,512]{1,0:T(8,128)(2,1)S(1)}, bf16[896,512]{1,0:T(8,128)(2,1)S(1)}, u32[]{:S(2)}, u32[]{:S(2)}) %collective-permute-start.16) | collective-permute-done | bytes 917536 | tf_op jit(solution)/shard_map/ppermute | solution.py:41
  209.2 20.1 %collective-permute-done.15 = bf16[896,512]{1,0:T(8,128)(2,1)S(1)} collective-permute-done((bf16[896,512]{1,0:T(8,128)(2,1)S(1)}, bf16[896,512]{1,0:T(8,128)(2,1)S(1)}, u32[]{:S(2)}, u32[]{:S(2)}) %collective-permute-start.15) | collective-permute-done | bytes 917536 | tf_op jit(solution)/shard_map/ppermute | solution.py:41
  230.0 2.5 collective-permute-start.19
  233.4 14.6 %collective-permute-done.10 = bf16[912,512]{1,0:T(8,128)(2,1)S(1)} collective-permute-done((bf16[912,512]{1,0:T(8,128)(2,1)S(1)}, bf16[912,512]{1,0:T(8,128)(2,1)S(1)}, u32[]{:S(2)}, u32[]{:S(2)}) %collective-permute-start.10) | collective-permute-done | bytes 933920 | tf_op jit(solution)/shard_map/ppermute | solution.py:41
  249.3 19.4 %collective-permute-done.9 = bf16[912,512]{1,0:T(8,128)(2,1)S(1)} collective-permute-done((bf16[912,512]{1,0:T(8,128)(2,1)S(1)}, bf16[912,512]{1,0:T(8,128)(2,1)S(1)}, u32[]{:S(2)}, u32[]{:S(2)}) %collective-permute-start.9) | collective-permute-done | bytes 933920 | tf_op jit(solution)/shard_map/ppermute | solution.py:41
  270.1 2.3 collective-permute-start.13
  273.3 2.7 collective-permute-start.11
  277.4 8.5 %collective-permute-done.13 = bf16[240,512]{1,0:T(8,128)(2,1)S(1)} collective-permute-done((bf16[240,512]{1,0:T(8,128)(2,1)S(1)}, bf16[240,512]{1,0:T(8,128)(2,1)S(1)}, u32[]{:S(2)}, u32[]{:S(2)}) %collective-permute-start.13) | collective-permute-done | bytes 245792 | tf_op jit(solution)/shard_map/ppermute | solution.py:45
  285.9 4.3 %collective-permute-done.12 = bf16[240,512]{1,0:T(8,128)(2,1)S(1)} collective-permute-done((bf16[240,512]{1,0:T(8,128)(2,1)S(1)}, bf16[240,512]{1,0:T(8,128)(2,1)S(1)}, u32[]{:S(2)}, u32[]{:S(2)}) %collective-permute-start.12) | collective-permute-done | bytes 245792 | tf_op jit(solution)/shard_map/ppermute | solution.py:45
  290.3 6.1 %collective-permute-done.11 = bf16[240,512]{1,0:T(8,128)(2,1)S(1)} collective-permute-done((bf16[240,512]{1,0:T(8,128)(2,1)S(1)}, bf16[240,512]{1,0:T(8,128)(2,1)S(1)}, u32[]{:S(2)}, u32[]{:S(2)}) %collective-permute-start.11) | collective-permute-done | bytes 245792 | tf_op jit(solution)/shard_map/ppermute | solution.py:45
  296.5 2.7 divide_subtract_fusion.1
  (108 shorter events, 27.7 us)
Async XLA Ops:
  7.2 98.4 %all-gather.2.cloned.1.call-start = ((), (), s32[]{:S(2)}) async-start(), calls=%async_computation.2 | async-start | bytes 3899392 | tf_op jit(solution)/shard_map/all_gather | solution.py:111
  9.2 10.7 %collective-permute-start = (bf16[224,512]{1,0:T(8,128)(2,1)S(1)}, bf16[224,512]{1,0:T(8,128)(2,1)S(1)}, u32[]{:S(2)}, u32[]{:S(2)}) collective-permute-start(bf16[224,512]{1,0:T(8,128)(2,1)S(1)} %get-tuple-element.29), channel_id=1, source_target_pairs={{0,48},{16,0},{32,16},{48,32},{64,112},{80,64},{96,80},{112,96},{1... | collective-permute-start | bytes 688136 | tf_op jit(solution)/shard_map/ppermute | solution.py:45
  9.3 23.4 %collective-permute-start.1 = (bf16[224,512]{1,0:T(8,128)(2,1)S(1)}, bf16[224,512]{1,0:T(8,128)(2,1)S(1)}, u32[]{:S(2)}, u32[]{:S(2)}) collective-permute-start(bf16[224,512]{1,0:T(8,128)(2,1)S(1)} %get-tuple-element.29), channel_id=1, source_target_pairs={{0,16},{16,32},{32,48},{48,0},{64,80},{80,96},{96,112},{112,64},{1... | collective-permute-start | bytes 688136 | tf_op jit(solution)/shard_map/ppermute | solution.py:45
  12.9 19.9 %collective-permute-start.2 = (bf16[224,512]{1,0:T(8,128)(2,1)S(1)}, bf16[224,512]{1,0:T(8,128)(2,1)S(1)}, u32[]{:S(2)}, u32[]{:S(2)}) collective-permute-start(bf16[224,512]{1,0:T(8,128)(2,1)S(1)} %get-tuple-element.29), channel_id=1, source_target_pairs={{0,32},{16,48},{32,0},{48,16},{64,96},{80,112},{96,64},{112,80},{1... | collective-permute-start | bytes 688136 | tf_op jit(solution)/shard_map/ppermute | solution.py:45
  32.8 24.2 %collective-permute-start.5 = (bf16[896,512]{1,0:T(8,128)(2,1)S(1)}, bf16[896,512]{1,0:T(8,128)(2,1)}, u32[]{:S(2)}, u32[]{:S(2)}) collective-permute-start(bf16[896,512]{1,0:T(8,128)(2,1)S(1)} %constant_dynamic-update-slice_fusion.2), channel_id=1, source_target_pairs={{0,128},{16,144},{32,160},{48,176},{64,192},{80,208},{96,224},{112... | collective-permute-start | bytes 2752520 | tf_op jit(solution)/shard_map/ppermute | solution.py:41
  33.9 42.0 %collective-permute-start.4 = (bf16[896,512]{1,0:T(8,128)(2,1)S(1)}, bf16[896,512]{1,0:T(8,128)(2,1)S(1)}, u32[]{:S(2)}, u32[]{:S(2)}) collective-permute-start(bf16[896,512]{1,0:T(8,128)(2,1)S(1)} %constant_dynamic-update-slice_fusion.2), channel_id=1, source_target_pairs={{0,64},{16,80},{32,96},{48,112},{64,128},{80,144},{96,160},{112,17... | collective-permute-start | bytes 2752520 | tf_op jit(solution)/shard_map/ppermute | solution.py:41
  35.7 45.6 %collective-permute-start.3 = (bf16[896,512]{1,0:T(8,128)(2,1)S(1)}, bf16[896,512]{1,0:T(8,128)(2,1)S(1)}, u32[]{:S(2)}, u32[]{:S(2)}) collective-permute-start(bf16[896,512]{1,0:T(8,128)(2,1)S(1)} %constant_dynamic-update-slice_fusion.2), channel_id=1, source_target_pairs={{0,192},{16,208},{32,224},{48,240},{64,0},{80,16},{96,32},{112,48}... | collective-permute-start | bytes 2752520 | tf_op jit(solution)/shard_map/ppermute | solution.py:41
  57.0 24.3 %copy-start.8 = (bf16[512,3584]{1,0:T(8,128)(2,1)S(1)}, bf16[512,3584]{1,0:T(8,128)(2,1)}, u32[]{:S(2)}) copy-start(bf16[512,3584]{1,0:T(8,128)(2,1)} %param.13) | copy-start | bytes 11010052
  77.8 4.3 %copy-start.15 = (f32[512]{0:T(512)S(1)}, f32[512]{0:T(512)}, u32[]{:S(2)}) copy-start(f32[512]{0:T(512)} %param.16) | copy-start | bytes 6148
  82.9 30.9 %copy-start.4 = (bf16[512,512]{1,0:T(8,128)(2,1)}, bf16[512,512]{1,0:T(8,128)(2,1)S(1)}, u32[]{:S(2)}) copy-start(bf16[512,512]{1,0:T(8,128)(2,1)S(1)} %get-tuple-element.22) | copy-start | bytes 1572868
  109.5 4.3 %collective-permute-start.6 = (bf16[1792,512]{1,0:T(8,128)(2,1)}, bf16[1792,512]{1,0:T(8,128)(2,1)}, u32[]{:S(2)}, u32[]{:S(2)}) collective-permute-start(bf16[1792,512]{1,0:T(8,128)(2,1)} %convolution_convert_fusion), channel_id=1, source_target_pairs={{0,1},{1,0},{2,3},{3,2},{4,5},{5,4},{6,7},{7,6},{8,9},{9,8},{10,11... | collective-permute-start | bytes 5505032 | tf_op jit(solution)/shard_map/ppermute | solution.py:49
  118.2 6.7 %copy-start.12 = (f32[3584]{0:T(1024)S(1)}, f32[3584]{0:T(1024)}, u32[]{:S(2)}) copy-start(f32[3584]{0:T(1024)} %param.17) | copy-start | bytes 43012
  118.2 28.5 %all-to-all-start = ((bf16[8,224,512]{2,1,0:T(8,128)(2,1)}), bf16[8,224,512]{2,1,0:T(8,128)(2,1)S(1)}, u32[]{:S(2)}, u32[]{:S(2)}) async-start(bf16[8,224,512]{2,1,0:T(8,128)(2,1)} %bitcast.28), calls=%async_computation | async-start | bytes 3670016 | tf_op jit(solution)/shard_map/all_to_all | solution.py:53
  147.3 28.2 %copy-start.2 = (bf16[3584,512]{1,0:T(8,128)(2,1)S(1)}, bf16[3584,512]{1,0:T(8,128)(2,1)}, u32[]{:S(2)}) copy-start(bf16[3584,512]{1,0:T(8,128)(2,1)} %all-gather.2.cloned.1.call-done) | copy-start | bytes 11010052
  173.1 5.8 %collective-permute-start.7 = (bf16[1792,512]{1,0:T(8,128)(2,1)S(1)}, bf16[1792,512]{1,0:T(8,128)(2,1)S(1)}, u32[]{:S(2)}, u32[]{:S(2)}) collective-permute-start(bf16[1792,512]{1,0:T(8,128)(2,1)S(1)} %bitcast.25), channel_id=1, source_target_pairs={{0,1},{1,0},{2,3},{3,2},{4,5},{5,4},{6,7},{7,6},{8,9},{9,8},{10,11... | collective-permute-start | bytes 5505032 | tf_op jit(solution)/shard_map/ppermute | solution.py:49
  182.8 3.5 %copy-start.1 = (bf16[3584,512]{1,0:T(8,128)(2,1)S(1)}, bf16[3584,512]{1,0:T(8,128)(2,1)}, u32[]{:S(2)}) copy-start(bf16[3584,512]{1,0:T(8,128)(2,1)} %copy-done) | copy-start | bytes 11010052
  185.1 23.2 %collective-permute-start.16 = (bf16[896,512]{1,0:T(8,128)(2,1)S(1)}, bf16[896,512]{1,0:T(8,128)(2,1)S(1)}, u32[]{:S(2)}, u32[]{:S(2)}) collective-permute-start(bf16[896,512]{1,0:T(8,128)(2,1)S(1)} %add_convert_fusion.1), channel_id=1, source_target_pairs={{0,128},{16,144},{32,160},{48,176},{64,192},{80,208},{96,224},{112... | collective-permute-start | bytes 2752520 | tf_op jit(solution)/shard_map/ppermute | solution.py:41
  188.2 3.5 %copy-start.9 = (bf16[512,3584]{1,0:T(8,128)(2,1)S(1)}, bf16[512,3584]{1,0:T(8,128)(2,1)}, u32[]{:S(2)}) copy-start(bf16[512,3584]{1,0:T(8,128)(2,1)} %param.13) | copy-start | bytes 11010052
  188.2 41.1 %collective-permute-start.15 = (bf16[896,512]{1,0:T(8,128)(2,1)S(1)}, bf16[896,512]{1,0:T(8,128)(2,1)S(1)}, u32[]{:S(2)}, u32[]{:S(2)}) collective-permute-start(bf16[896,512]{1,0:T(8,128)(2,1)S(1)} %add_convert_fusion.2), channel_id=1, source_target_pairs={{0,192},{16,208},{32,224},{48,240},{64,0},{80,16},{96,32},{112,48}... | collective-permute-start | bytes 2752520 | tf_op jit(solution)/shard_map/ppermute | solution.py:41
  188.9 40.4 %collective-permute-start.14 = (bf16[896,512]{1,0:T(8,128)(2,1)S(1)}, bf16[896,512]{1,0:T(8,128)(2,1)S(1)}, u32[]{:S(2)}, u32[]{:S(2)}) collective-permute-start(bf16[896,512]{1,0:T(8,128)(2,1)S(1)} %add_convert_fusion.3), channel_id=1, source_target_pairs={{0,64},{16,80},{32,96},{48,112},{64,128},{80,144},{96,160},{112,17... | collective-permute-start | bytes 2752520 | tf_op jit(solution)/shard_map/ppermute | solution.py:41
  193.2 54.8 %collective-permute-start.10 = (bf16[912,512]{1,0:T(8,128)(2,1)S(1)}, bf16[912,512]{1,0:T(8,128)(2,1)S(1)}, u32[]{:S(2)}, u32[]{:S(2)}) collective-permute-start(bf16[912,512]{1,0:T(8,128)(2,1)S(1)} %get-tuple-element.41), channel_id=1, source_target_pairs={{0,128},{16,144},{32,160},{48,176},{64,192},{80,208},{96,224},{112... | collective-permute-start | bytes 2801672 | tf_op jit(solution)/shard_map/ppermute | solution.py:41
  194.0 74.7 %collective-permute-start.9 = (bf16[912,512]{1,0:T(8,128)(2,1)S(1)}, bf16[912,512]{1,0:T(8,128)(2,1)S(1)}, u32[]{:S(2)}, u32[]{:S(2)}) collective-permute-start(bf16[912,512]{1,0:T(8,128)(2,1)S(1)} %get-tuple-element.40), channel_id=1, source_target_pairs={{0,192},{16,208},{32,224},{48,240},{64,0},{80,16},{96,32},{112,48}... | collective-permute-start | bytes 2801672 | tf_op jit(solution)/shard_map/ppermute | solution.py:41
  208.3 60.6 %collective-permute-start.8 = (bf16[912,512]{1,0:T(8,128)(2,1)S(1)}, bf16[912,512]{1,0:T(8,128)(2,1)S(1)}, u32[]{:S(2)}, u32[]{:S(2)}) collective-permute-start(bf16[912,512]{1,0:T(8,128)(2,1)S(1)} %get-tuple-element.39), channel_id=1, source_target_pairs={{0,64},{16,80},{32,96},{48,112},{64,128},{80,144},{96,160},{112,17... | collective-permute-start | bytes 2801672 | tf_op jit(solution)/shard_map/ppermute | solution.py:41
  230.0 43.2 %collective-permute-start.19 = (bf16[224,512]{1,0:T(8,128)(2,1)S(1)}, bf16[224,512]{1,0:T(8,128)(2,1)S(1)}, u32[]{:S(2)}, u32[]{:S(2)}) collective-permute-start(bf16[224,512]{1,0:T(8,128)(2,1)S(1)} %get-tuple-element.31), channel_id=1, source_target_pairs={{0,32},{16,48},{32,0},{48,16},{64,96},{80,112},{96,64},{112,80},{1... | collective-permute-start | bytes 688136 | tf_op jit(solution)/shard_map/ppermute | solution.py:45
  232.6 43.4 %collective-permute-start.18 = (bf16[224,512]{1,0:T(8,128)(2,1)S(1)}, bf16[224,512]{1,0:T(8,128)(2,1)S(1)}, u32[]{:S(2)}, u32[]{:S(2)}) collective-permute-start(bf16[224,512]{1,0:T(8,128)(2,1)S(1)} %get-tuple-element.32), channel_id=1, source_target_pairs={{0,48},{16,0},{32,16},{48,32},{64,112},{80,64},{96,80},{112,96},{1... | collective-permute-start | bytes 688136 | tf_op jit(solution)/shard_map/ppermute | solution.py:45
  248.0 28.0 %collective-permute-start.17 = (bf16[224,512]{1,0:T(8,128)(2,1)S(1)}, bf16[224,512]{1,0:T(8,128)(2,1)S(1)}, u32[]{:S(2)}, u32[]{:S(2)}) collective-permute-start(bf16[224,512]{1,0:T(8,128)(2,1)S(1)} %get-tuple-element.30), channel_id=1, source_target_pairs={{0,16},{16,32},{32,48},{48,0},{64,80},{80,96},{96,112},{112,64},{1... | collective-permute-start | bytes 688136 | tf_op jit(solution)/shard_map/ppermute | solution.py:45
  269.9 6.1 %copy-start.7 = (f32[224,512]{1,0:T(8,128)S(1)}, f32[224,512]{1,0:T(8,128)}, u32[]{:S(2)}) copy-start(f32[224,512]{1,0:T(8,128)} %param.15) | copy-start | bytes 1376260
  269.9 6.1 %copy-start.10 = (f32[224,512]{1,0:T(8,128)S(1)}, f32[224,512]{1,0:T(8,128)}, u32[]{:S(2)}) copy-start(f32[224,512]{1,0:T(8,128)} %param.20) | copy-start | bytes 1376260
  269.9 6.1 %copy-start.11 = (f32[224,512]{1,0:T(8,128)S(1)}, f32[224,512]{1,0:T(8,128)}, u32[]{:S(2)}) copy-start(f32[224,512]{1,0:T(8,128)} %param.21) | copy-start | bytes 1376260
  270.1 15.8 %collective-permute-start.13 = (bf16[240,512]{1,0:T(8,128)(2,1)S(1)}, bf16[240,512]{1,0:T(8,128)(2,1)S(1)}, u32[]{:S(2)}, u32[]{:S(2)}) collective-permute-start(bf16[240,512]{1,0:T(8,128)(2,1)S(1)} %get-tuple-element.38), channel_id=1, source_target_pairs={{0,32},{16,48},{32,0},{48,16},{64,96},{80,112},{96,64},{112,80},{1... | collective-permute-start | bytes 737288 | tf_op jit(solution)/shard_map/ppermute | solution.py:45
  272.4 17.8 %collective-permute-start.12 = (bf16[240,512]{1,0:T(8,128)(2,1)S(1)}, bf16[240,512]{1,0:T(8,128)(2,1)S(1)}, u32[]{:S(2)}, u32[]{:S(2)}) collective-permute-start(bf16[240,512]{1,0:T(8,128)(2,1)S(1)} %get-tuple-element.37), channel_id=1, source_target_pairs={{0,48},{16,0},{32,16},{48,32},{64,112},{80,64},{96,80},{112,96},{1... | collective-permute-start | bytes 737288 | tf_op jit(solution)/shard_map/ppermute | solution.py:45
  273.3 23.1 %collective-permute-start.11 = (bf16[240,512]{1,0:T(8,128)(2,1)S(1)}, bf16[240,512]{1,0:T(8,128)(2,1)S(1)}, u32[]{:S(2)}, u32[]{:S(2)}) collective-permute-start(bf16[240,512]{1,0:T(8,128)(2,1)S(1)} %get-tuple-element.36), channel_id=1, source_target_pairs={{0,16},{16,32},{32,48},{48,0},{64,80},{80,96},{96,112},{112,64},{1... | collective-permute-start | bytes 737288 | tf_op jit(solution)/shard_map/ppermute | solution.py:45
  (8 other events, 21.2 us)
Sparse Core Ops, SparseCore 0:
  11.1 94.5 all-gather.1
